TPU v7x, 32 devices: a whole 2x2x4 slice. The times are simulated.
32 devices in a mesh: grp: 2 (over x), ex: 16 (over z, y, core).
Axes of the slice: x: 2, y: 2, z: 4, core: 2. Of those that a mesh axis runs over, the one named last changes fastest.
Arguments:
- queries: bfloat16 [256, 4096], P(('grp', 'ex')), parts along dimension 0, may hold values from -6 to 6
- train_grads: bfloat16 [32768, 4096], P(('grp', 'ex')), parts along dimension 0
Outputs:
- scores: float32 [128, 32768], P(None, ('grp', 'ex')), parts along dimension 1
- best_scores: float32 [256, 8], P(('grp', 'ex')), parts along dimension 0
There are 2 independent parts, one for each index of `grp`. A program takes and returns all parts, laid end to end along the dimension named above; each array names one. Nothing has to cross between parts.
All inputs are finite; a program needn't handle non-finite values.
Results may differ from a plain program's by a relative error of at most 0.0003.
Values may be sent and summed in bfloat16 or wider, within the bound.
A program may use at most 192 MiB of HBM per device.

v0:
```python
import jax
import jax.numpy as jnp
from jax import lax
from jax.sharding import PartitionSpec as P

TOPV = 8


def shards(queries, train_grads):
    width = train_grads.shape[1]
    squares = jnp.square(train_grads.astype(jnp.float32))
    scale = lax.rsqrt(jnp.mean(squares, axis=1) + 1e-06) / jnp.sqrt(jnp.float32(width))
    gathered = lax.all_gather(queries, "ex", axis=0, tiled=True)
    raw = lax.dot_general(
        gathered, train_grads, (((1,), (1,)), ((), ())), preferred_element_type=jnp.float32
    )
    scores = raw * scale[None, :]
    local_best = lax.top_k(scores, TOPV)[0]
    own_rows = queries.shape[0]
    everything = lax.all_gather(local_best[None], "ex", axis=0, tiled=True)
    mine = lax.dynamic_slice_in_dim(everything, lax.axis_index("ex") * own_rows, own_rows, 1)
    candidates = jnp.moveaxis(mine, 0, 1).reshape(own_rows, -1)
    best_scores = lax.top_k(candidates, TOPV)[0]
    return (scores, best_scores)


def solution(mesh):
    in_specs = (P(("grp", "ex"), None), P(("grp", "ex"), None))
    out_specs = (P(None, ("grp", "ex")), P(("grp", "ex"), None))
    return jax.shard_map(shards, mesh=mesh, in_specs=in_specs, out_specs=out_specs, check_vma=False)
```

profile of v0, /device:TPU:0, one launch (start us, length us, event | category | flops | bytes accessed | tf_op | source)
XLA Modules:
  0.0 120.7 jit_solution(16510975565905021380)
XLA Ops:
  7.2 0.0 all-gather.3.cloned.1.call-start
  7.2 0.7 all-gather.3.cloned.1.call-update
  7.9 5.1 %multiply_reduce_fusion = f32[1024]{0:T(1024)S(1)} fusion(bf16[1024,4096]{1,0:T(8,128)(2,1)} %param.3), kind=kLoop, calls=%fused_computation | loop fusion | flops 12581888 | bytes 8392704 | tf_op jit(solution)/shard_map/reduce_sum | solution.py:12
  13.0 37.8 %all-gather.3.cloned.1.call-done = bf16[128,4096]{1,0:T(8,128)(2,1)} async-done(((bf16[8,4096]{1,0:T(8,128)(2,1)}), bf16[128,4096]{1,0:T(8,128)(2,1)}) %all-gather.3.cloned.1.call-update) | async-done | bytes 1048592 | tf_op jit(solution)/shard_map/all_gather | solution.py:13
  50.8 6.6 %convolution_multiply_fusion = f32[128,1024]{1,0:T(8,128)S(1)} fusion(bf16[128,4096]{1,0:T(8,128)(2,1)} %all-gather.3.cloned.1.call-done, bf16[1024,4096]{1,0:T(8,128)(2,1)} %param.3, f32[1024]{0:T(1024)S(1)} %rsqrt_multiply_fusion), kind=kOutput, calls=%fused_computation.1 | convolution fusion | flops 1073872896 | bytes 9965568 | tf_op jit(solution)/shard_map/dot_general | solution.py:14
  57.5 0.0 copy-start
  57.5 31.4 %top_k.13 = (f32[128,8]{1,0:T(8,128)S(1)}, s32[128,8]{1,0:T(8,128)}) custom-call(f32[128,1024]{1,0:T(8,128)S(1)} %convolution_multiply_fusion), custom_call_target="TopK", called_computations={%compare_greater_than.1.2.clone.clone} | custom-call | tf_op jit(solution)/shard_map/top_k | solution.py:18
  88.8 22.2 %all-gather = f32[2048,8]{1,0:T(8,128)S(1)} all-gather(f32[128,8]{1,0:T(8,128)S(1)} %get-tuple-element.7), channel_id=2, replica_groups=mesh['grp'=2,'ex'=16] {'ex'}, dimensions={0}, use_global_device_ids=true | all-gather | bytes 69632 | tf_op jit(solution)/shard_map/all_gather | solution.py:20
  111.1 0.1 reshape.13
  111.2 2.6 %top_k.14 = (f32[8,128]{1,0:T(8,128)}, s32[8,128]{1,0:T(8,128)}) sort(f32[8,128]{1,0:T(8,128)S(1)} %reshape.13, s32[8,128]{1,0:T(8,128)S(1)} %iota.3), dimensions={1}, to_apply=%region_1.3 | sort | flops 10240 | bytes 16384 | tf_op jit(solution)/shard_map/top_k | solution.py:23
  113.8 0.0 copy-done
  (4 shorter events, 0.0 us)
Async XLA Ops:
  7.2 43.7 %all-gather.3.cloned.1.call-start = ((), (), s32[]{:S(2)}) async-start(), calls=%async_computation | async-start | bytes 1114112 | tf_op jit(solution)/shard_map/all_gather | solution.py:13
  57.5 56.4 %copy-start = (f32[128,1024]{1,0:T(8,128)}, f32[128,1024]{1,0:T(8,128)S(1)}, u32[]{:S(2)}) copy-start(f32[128,1024]{1,0:T(8,128)S(1)} %convolution_multiply_fusion) | copy-start | bytes 1572868
Sparse Core Ops, SparseCore 0:
  10.2 40.6 all-gather.2
where the time goes:
time: 121 us
  other arithmetic  39.1 us (32%)
  waiting for transfers between devices  38.5 us (32%)
  blocking collectives  22.2 us (18%)
  between operations  14.1 us (12%)
  matrix products  6.62 us (5%)
    all_gather x1, waiting for transfers between devices, shards(): gathered = lax.all_gather(queries, 'ex', axis=0, tiled=True)  37.8 us
    top_k x1, other arithmetic, shards(): local_best = lax.top_k(scores, TOPV)[0]  31.4 us
    all_gather x1, blocking collectives, shards(): everything = lax.all_gather(local_best[None], 'ex', axis=0, tiled=True)  22.2 us
    dot_general x1, matrix products, shards(): lax.dot_general(gathered, train_grads, (((1,), (1,)), ((), ())), preferre...  6.62 us
    reduce_sum x1, other arithmetic, shards(): jnp.mean(squares, axis=1) + 1e-06  5.07 us
    top_k x1, other arithmetic, shards(): best_scores = lax.top_k(candidates, TOPV)[0]  2.64 us
  transfers between devices with their start and end apart: 1, of which 1 were waited for; matrix products, arithmetic and copies ran while one was open for 4% of the time, Pallas kernels for 0%

commit v1 on v0

v1 whole, which is shorter than its diff:
```python
import functools

import jax
import jax.numpy as jnp
from jax import lax
from jax.experimental import pallas as pl
from jax.experimental.pallas import tpu as pltpu
from jax.sharding import PartitionSpec as P

TOPV = 8
LANES = 128
CHUNKS = 4
SORT8 = (
    (0, 1), (2, 3), (4, 5), (6, 7), (0, 2), (1, 3), (4, 6), (5, 7), (1, 2), (5, 6),
    (0, 4), (1, 5), (2, 6), (3, 7), (2, 4), (3, 5), (1, 2), (3, 4), (5, 6),
)
MERGE8 = (
    (0, 4), (1, 5), (2, 6), (3, 7), (0, 2), (1, 3), (4, 6), (5, 7), (0, 1), (2, 3), (4, 5), (6, 7),
)


def network(rows, pairs):
    rows = list(rows)
    for i, j in pairs:
        rows[i], rows[j] = jnp.maximum(rows[i], rows[j]), jnp.minimum(rows[i], rows[j])
    return rows


def merge(left, right):
    return network([jnp.maximum(left[i], right[TOPV - 1 - i]) for i in range(TOPV)], MERGE8)


def over_sublanes(best):
    for shift in (4, 2, 1):
        best = merge(best, [pltpu.roll(row, shift, 0) for row in best])
    place = lax.broadcasted_iota(jnp.int32, best[0].shape, 0)
    tile = best[0]
    for i in range(1, TOPV):
        tile = jnp.where(place == i, best[i], tile)
    return tile


def each(count, body):
    if count <= 16:
        for i in range(count):
            body(i)
    else:
        lax.fori_loop(0, count, lambda i, _: (body(i), None)[1], None)


def kernel(
    outer, inner, q_ref, t_ref, scores_ref, best_ref,
    qbuf, tbuf, squares, scale, acc, outbuf, tile, tiles, turned,
    t_sem, own_sem, out_sem, recv_sem, send_z, send_y, send_c, tile_send, tile_recv,
):
    ex = 2 * outer * inner
    own, width = q_ref.shape
    rows = t_ref.shape[0]
    nq = ex * own
    groups = nq // LANES
    kc = width // CHUNKS
    me = lax.axis_index("ex")
    core = lax.rem(me, 2)
    chip = me // 2
    a, b = chip // inner, lax.rem(chip, inner)

    def at(aa, bb, cc):
        return (aa * inner + bb) * 2 + cc

    def columns(k):
        return pl.ds(k * kc, kc)

    t_copies = []
    for k in range(CHUNKS):
        copy = pltpu.make_async_copy(t_ref.at[:, columns(k)], tbuf.at[k], t_sem.at[k])
        copy.start()
        t_copies.append(copy)
    own_copies = []
    for k in range(CHUNKS):
        copy = pltpu.make_async_copy(q_ref.at[:, columns(k)], qbuf.at[k, me], own_sem.at[k])
        copy.start()
        own_copies.append(copy)

    barrier = pltpu.get_barrier_semaphore()

    def greet(i):
        pl.semaphore_signal(
            barrier, inc=1, device_id={"ex": lax.rem(me + 1 + i, ex)},
            device_id_type=pl.DeviceIdType.MESH,
        )

    each(ex - 1, greet)
    pl.semaphore_wait(barrier, ex - 1)

    def remote(k, slot, target, send, src=None):
        return pltpu.make_async_remote_copy(
            src_ref=qbuf.at[k, slot] if src is None else src,
            dst_ref=qbuf.at[k, slot],
            send_sem=send,
            recv_sem=recv_sem.at[k, slot],
            device_id={"ex": target},
            device_id_type=pl.DeviceIdType.MESH,
        )

    def z_copy(k, i):
        aa = lax.rem(a + 1 + i, outer)
        return remote(k, me, at(aa, b, core), send_z.at[k, i], q_ref.at[:, columns(k)])

    def y_copy(k, i, j):
        aa, bb = lax.rem(a + i, outer), lax.rem(b + 1 + j, inner)
        src = q_ref.at[:, columns(k)] if isinstance(i, int) and i == 0 else None
        return remote(k, at(aa, b, core), at(a, bb, core), send_y.at[k, i, j], src)

    def c_copy(k, i, j):
        aa, bb = lax.rem(a + i, outer), lax.rem(b + j, inner)
        src = q_ref.at[:, columns(k)] if isinstance(i, int) and isinstance(j, int) and i == j == 0 else None
        return remote(k, at(aa, bb, core), at(a, b, 1 - core), send_c.at[k, i, j], src)

    def arrived(k, slot):
        remote(k, slot, me, own_sem.at[k]).wait_recv()

    for k in range(CHUNKS):
        each(outer - 1, lambda i: z_copy(k, i).start())
        each(inner - 1, lambda j: y_copy(k, 0, j).start())
        c_copy(k, 0, 0).start()

    def pass_z(k):
        def one(i):
            arrived(k, at(lax.rem(a + 1 + i, outer), b, core))
            each(inner - 1, lambda j: y_copy(k, i + 1, j).start())
            c_copy(k, i + 1, 0).start()
        each(outer - 1, one)

    def pass_y(k):
        def one(i):
            def two(j):
                arrived(k, at(lax.rem(a + i, outer), lax.rem(b + 1 + j, inner), core))
                c_copy(k, i, j + 1).start()
            each(inner - 1, two)
        each(outer, one)

    def pass_c(k):
        def one(i):
            each(inner, lambda j: arrived(k, at(lax.rem(a + i, outer), lax.rem(b + j, inner), 1 - core)))
        each(outer, one)
        own_copies[k].wait()

    def square(k):
        t_copies[k].wait()
        block = 64

        def one(r, _):
            here = pl.ds(pl.multiple_of(r * block, block), block)
            total = None
            for g in range(kc // LANES):
                x = tbuf[k, here, pl.ds(g * LANES, LANES)].astype(jnp.float32)
                total = x * x if total is None else total + x * x
            if k:
                total = total + squares[here, :]
            if k < CHUNKS - 1:
                squares[here, :] = total
            else:
                mean = jnp.sum(total, axis=1, keepdims=True) * jnp.float32(1.0 / width)
                factor = lax.rsqrt(mean + 1e-06) * jnp.float32(width ** -0.5)
                scale[here, :] = jnp.broadcast_to(factor, (block, LANES))

        lax.fori_loop(0, rows // block, one, None)

    def query_block(k, g):
        per = LANES // own
        return qbuf[k, pl.ds(g * per, per)].reshape(LANES, kc)

    def product(k, here, g):
        return lax.dot_general(
            tbuf[k, here, :], query_block(k, g), (((1,), (1,)), ((), ())),
            preferred_element_type=jnp.float32,
        )

    def multiply(k):
        def one(g):
            new = product(k, slice(None), g)
            acc[g] = new if k == 0 else acc[g] + new
        each(groups, one)

    step = 256
    out_copies = []

    def last(g):
        best = None
        for r in range(rows // step):
            here = pl.ds(r * step, step)
            value = (acc[g, here, :] + product(CHUNKS - 1, here, g)) * scale[here, :]
            for s in range(step // LANES):
                outbuf[pl.ds(g * LANES, LANES), pl.ds(r * step + s * LANES, LANES)] = (
                    value[s * LANES:(s + 1) * LANES].T
                )
            for s in range(step // 64):
                lists = network([value[s * 64 + i * 8:s * 64 + i * 8 + 8] for i in range(8)], SORT8)
                best = lists if best is None else merge(best, lists)
        tile[g] = over_sublanes(best)

    for t in range(CHUNKS + 2):
        if t < CHUNKS:
            pass_z(t)
        if 0 <= t - 1 < CHUNKS:
            pass_y(t - 1)
        if t < CHUNKS:
            square(t)
        k = t - 2
        if 0 <= k < CHUNKS:
            pass_c(k)
            if k < CHUNKS - 1:
                multiply(k)
            else:
                each(groups, last)

    def tile_copy(i):
        target = lax.rem(me + 1 + i, ex)
        return pltpu.make_async_remote_copy(
            src_ref=tile.at[target * own // LANES],
            dst_ref=tiles.at[me],
            send_sem=tile_send.at[i],
            recv_sem=tile_recv.at[me],
            device_id={"ex": target},
            device_id_type=pl.DeviceIdType.MESH,
        )

    each(ex - 1, lambda i: tile_copy(i).start())
    out = pltpu.make_async_copy(outbuf, scores_ref, out_sem)
    out.start()
    tiles[me] = tile[me * own // LANES]

    def tile_wait(i):
        source = lax.rem(me + 1 + i, ex)
        pltpu.make_async_remote_copy(
            src_ref=tile.at[0], dst_ref=tiles.at[source], send_sem=tile_send.at[i],
            recv_sem=tile_recv.at[source], device_id={"ex": source},
            device_id_type=pl.DeviceIdType.MESH,
        ).wait_recv()

    each(ex - 1, tile_wait)
    best = None
    for s in range(ex // 8):
        lists = network([tiles[s * 8 + i] for i in range(8)], SORT8)
        best = lists if best is None else merge(best, lists)
    turned[...] = over_sublanes(best).T
    best_ref[...] = turned[pl.ds(pl.multiple_of(lax.rem(me * own, LANES), own), own), :]

    each(ex - 1, lambda i: tile_copy(i).wait_send())
    for k in range(CHUNKS):
        each(outer - 1, lambda i: z_copy(k, i).wait_send())
        each(outer, lambda i: each(inner - 1, lambda j: y_copy(k, i, j).wait_send()))
        each(outer, lambda i: each(inner, lambda j: c_copy(k, i, j).wait_send()))
    out.wait()


def shards(ex, queries, train_grads):
    own, width = queries.shape
    rows = train_grads.shape[0]
    nq = ex * own
    groups = nq // LANES
    kc = width // CHUNKS
    chips = ex // 2
    inner = 1
    while inner * inner * 4 <= chips:
        inner *= 2
    outer = chips // inner
    any_space = pl.BlockSpec(memory_space=pl.ANY)
    dma = pltpu.SemaphoreType.DMA
    return pl.pallas_call(
        functools.partial(kernel, outer, inner),
        out_shape=(
            jax.ShapeDtypeStruct((nq, rows), jnp.float32),
            jax.ShapeDtypeStruct((own, TOPV), jnp.float32),
        ),
        in_specs=[any_space, any_space],
        out_specs=(any_space, pl.BlockSpec(memory_space=pltpu.VMEM)),
        scratch_shapes=[
            pltpu.VMEM((CHUNKS, ex, own, kc), jnp.bfloat16),
            pltpu.VMEM((CHUNKS, rows, kc), jnp.bfloat16),
            pltpu.VMEM((rows, LANES), jnp.float32),
            pltpu.VMEM((rows, LANES), jnp.float32),
            pltpu.VMEM((groups, rows, LANES), jnp.float32),
            pltpu.VMEM((nq, rows), jnp.float32),
            pltpu.VMEM((groups, TOPV, LANES), jnp.float32),
            pltpu.VMEM((ex, TOPV, LANES), jnp.float32),
            pltpu.VMEM((LANES, TOPV), jnp.float32),
            dma((CHUNKS,)),
            dma((CHUNKS,)),
            dma,
            dma((CHUNKS, ex)),
            dma((CHUNKS, max(outer - 1, 1))),
            dma((CHUNKS, outer, max(inner - 1, 1))),
            dma((CHUNKS, outer, inner)),
            dma((ex,)),
            dma((ex,)),
        ],
        compiler_params=pltpu.CompilerParams(
            collective_id=0, has_side_effects=True, vmem_limit_bytes=48 * 1024 * 1024
        ),
    )(queries, train_grads)


def solution(mesh):
    in_specs = (P(("grp", "ex"), None), P(("grp", "ex"), None))
    out_specs = (P(None, ("grp", "ex")), P(("grp", "ex"), None))
    return jax.shard_map(
        functools.partial(shards, mesh.shape["ex"]),
        mesh=mesh, in_specs=in_specs, out_specs=out_specs, check_vma=False,
    )
```

time: 121 us -> 31.1 us (0.26)
  other arithmetic: 39.1 us -> 0 us
  waiting for transfers between devices: 38.5 us -> 0 us
  Pallas kernels: 0 us -> 28.1 us
  blocking collectives: 22.2 us -> 0 us
  between operations: 14.1 us -> 0.65 us
  matrix products: 6.62 us -> 0 us
  local copies, waits for them, and re-layouts: 0.13 us -> 2.22 us
    all_gather x1 -> x0, waiting for transfers between devices: 37.8 us -> none  [shards(): gathered = lax.all_gather(queries, 'ex', axis=0, tiled=True)]
    top_k x2 -> x0, other arithmetic: 34 us -> none  [the longest x1 31.4 us: shards(): local_best = lax.top_k(scores, TOPV)[0]]
    pallas_call x0 -> x1, Pallas kernels: none -> 28.1 us  [shards(): pl.pallas_call(functools.partial(kernel, outer, inner), out_shape=(jax.Sh...]
    all_gather x1 -> x0, blocking collectives: 22.2 us -> none  [shards(): everything = lax.all_gather(local_best[None], 'ex', axis=0, tiled=True)]
    dot_general x1 -> x0, matrix products: 6.62 us -> none  [shards(): lax.dot_general(gathered, train_grads, (((1,), (1,)), ((), ())), preferre...]
    reduce_sum x1 -> x0, other arithmetic: 5.07 us -> none  [shards(): jnp.mean(squares, axis=1) + 1e-06]
    unnamed x3 -> x4, local copies, waits for them, and re-layouts: 0.02 us -> 2.22 us
  transfers between devices with their start and end apart: 1 -> 0, of which waited for: 1 -> 0; matrix products, arithmetic and copies ran while one was open for 4% -> 0% of each run, Pallas kernels for 0% -> 0%
where the time goes in v1:
time: 31.1 us; the launch traced here: 30.9 us
  Pallas kernels  28.1 us (90%)
  local copies, waits for them, and re-layouts  2.22 us (7%)
  between operations  0.65 us (2%)
    pallas_call x1, Pallas kernels, shards(): pl.pallas_call(functools.partial(kernel, outer, inner), out_shape=(jax.Sh...  28.1 us
    unnamed x4, local copies, waits for them, and re-layouts  2.22 us

profile of v1, /device:TPU:0, one launch (start us, length us, event | category | flops | bytes accessed | tf_op | source)
XLA Modules:
  0.0 30.9 jit_solution(12564180896340092950)
XLA Ops:
  0.6 0.0 copy-start
  0.6 0.8 %copy-done = bf16[8,4096]{1,0:T(8,128)(2,1)S(1)} copy-done((bf16[8,4096]{1,0:T(8,128)(2,1)S(1)}, bf16[8,4096]{1,0:T(8,128)(2,1)}, u32[]{:S(2)}) %copy-start) | copy-done | bytes 65560
  1.5 28.1 %shard_map.41 = (f32[128,1024]{1,0:T(8,128)S(1)}, f32[8,8]{1,0:T(8,128)S(1)}) custom-call(bf16[8,4096]{1,0:T(8,128)(2,1)S(1)} %copy-done, bf16[1024,4096]{1,0:T(8,128)(2,1)} %t_ref.1), custom_call_target="tpu_custom_call" | custom-call | tf_op jit(solution)/shard_map/pallas_call | solution.py:270
  29.5 0.8 %copy.6 = f32[128,1024]{1,0:T(8,128)} copy(f32[128,1024]{1,0:T(8,128)S(1)} %get-tuple-element.4) | data formatting | bytes 1048576
  30.3 0.6 %copy.7 = f32[8,8]{1,0:T(8,128)} copy(f32[8,8]{1,0:T(8,128)S(1)} %get-tuple-element.5) | data formatting | bytes 512
Async XLA Ops:
  0.6 0.8 %copy-start = (bf16[8,4096]{1,0:T(8,128)(2,1)S(1)}, bf16[8,4096]{1,0:T(8,128)(2,1)}, u32[]{:S(2)}) copy-start(bf16[8,4096]{1,0:T(8,128)(2,1)} %q_ref.1) | copy-start | bytes 196612

commit v2 on v1

v2 whole, which is shorter than its diff:
```python
import functools

import jax
import jax.numpy as jnp
from jax import lax
from jax.experimental import pallas as pl
from jax.experimental.pallas import tpu as pltpu
from jax.sharding import PartitionSpec as P

TOPV = 8
LANES = 128
SHARES = (1, 1)
PER_EVENT = 4
VMEM_MIB = 48
SORT8 = (
    (0, 1), (2, 3), (4, 5), (6, 7), (0, 2), (1, 3), (4, 6), (5, 7), (1, 2), (5, 6),
    (0, 4), (1, 5), (2, 6), (3, 7), (2, 4), (3, 5), (1, 2), (3, 4), (5, 6),
)
MERGE8 = (
    (0, 4), (1, 5), (2, 6), (3, 7), (0, 2), (1, 3), (4, 6), (5, 7), (0, 1), (2, 3), (4, 5), (6, 7),
)


def network(rows, pairs):
    rows = list(rows)
    for i, j in pairs:
        rows[i], rows[j] = jnp.maximum(rows[i], rows[j]), jnp.minimum(rows[i], rows[j])
    return rows


def merge(left, right):
    return network([jnp.maximum(left[i], right[TOPV - 1 - i]) for i in range(TOPV)], MERGE8)


def over_sublanes(best):
    for shift in (4, 2, 1):
        best = merge(best, [pltpu.roll(row, shift, 0) for row in best])
    place = lax.broadcasted_iota(jnp.int32, best[0].shape, 0)
    tile = best[0]
    for i in range(1, TOPV):
        tile = jnp.where(place == i, best[i], tile)
    return tile


def each(count, body):
    if count <= 16:
        for i in range(count):
            body(i)
    else:
        lax.fori_loop(0, count, lambda i, _: (body(i), None)[1], None)


def kernel(outer, inner, widths, q_ref, t_ref, scores_ref, best_ref, *scratch):
    chunks = len(widths)
    qbufs, tbufs = scratch[:chunks], scratch[chunks:2 * chunks]
    (
        squares, scale, acc, tile, tiles, turned, t_sem, own_sem,
        z_send, z_recv, y_send, y_recv, c_send, c_recv, tile_send, tile_recv,
    ) = scratch[2 * chunks:]
    ex = 2 * outer * inner
    own, width = q_ref.shape
    rows = t_ref.shape[0]
    groups = ex * own // LANES
    starts = [sum(widths[:k]) for k in range(chunks)]
    me = lax.axis_index("ex")
    core = lax.rem(me, 2)
    chip = me // 2
    a, b = chip // inner, lax.rem(chip, inner)

    def at(aa, bb, cc):
        return (aa * inner + bb) * 2 + cc

    def own_block(k):
        return q_ref.at[:, pl.ds(starts[k], widths[k])]

    barrier = pltpu.get_barrier_semaphore()

    def greet(i):
        pl.semaphore_signal(
            barrier, inc=1, device_id={"ex": lax.rem(me + 1 + i, ex)},
            device_id_type=pl.DeviceIdType.MESH,
        )

    each(ex - 1, greet)
    t_copies = []
    for k in range(chunks):
        copy = pltpu.make_async_copy(t_ref.at[:, pl.ds(starts[k], widths[k])], tbufs[k], t_sem.at[k])
        copy.start()
        t_copies.append(copy)
    own_copies = []
    for k in range(chunks):
        copy = pltpu.make_async_copy(own_block(k), qbufs[k].at[core, b, a], own_sem.at[k])
        copy.start()
        own_copies.append(copy)
    pl.semaphore_wait(barrier, ex - 1)

    def remote(src, dst, send, recv, target):
        return pltpu.make_async_remote_copy(
            src_ref=src, dst_ref=dst, send_sem=send, recv_sem=recv,
            device_id={"ex": target}, device_id_type=pl.DeviceIdType.MESH,
        )

    def z_copy(k, i):
        target = at(lax.rem(a + 1 + i, outer), b, core)
        return remote(own_block(k), qbufs[k].at[core, b, a], z_send.at[k, i], z_recv.at[k, a], target)

    def y_copy(k, i, j):
        aa, bb = lax.rem(a + i, outer), lax.rem(b + 1 + j, inner)
        place = qbufs[k].at[core, b, aa]
        src = own_block(k) if isinstance(i, int) and i == 0 else place
        return remote(src, place, y_send.at[k, j, i], y_recv.at[k, b, aa], at(a, bb, core))

    def c_copy(k, j):
        bb = lax.rem(b + j, inner)
        place = qbufs[k].at[core, bb]
        return remote(place, place, c_send.at[k, j], c_recv.at[k, bb], at(a, b, 1 - core))

    def arrived(place, sem):
        remote(place, place, sem, sem, me).wait_recv()

    for k in range(chunks):
        each(outer - 1, lambda i: z_copy(k, i).start())
        each(inner - 1, lambda j: y_copy(k, 0, j).start())

    def pass_z(k):
        def one(i):
            aa = lax.rem(a + 1 + i, outer)
            arrived(qbufs[k].at[core, b, aa], z_recv.at[k, aa])
            each(inner - 1, lambda j: y_copy(k, i + 1, j).start())
        each(outer - 1, one)
        own_copies[k].wait()
        c_copy(k, 0).start()

    def pass_y(k):
        def two(j):
            bb = lax.rem(b + 1 + j, inner)
            each(outer, lambda aa: arrived(qbufs[k].at[core, bb, aa], y_recv.at[k, bb, aa]))
            c_copy(k, j + 1).start()
        each(inner - 1, two)

    def pass_c(k):
        each(inner, lambda bb: arrived(qbufs[k].at[1 - core, bb], c_recv.at[k, bb]))

    parts = 4
    block = 64

    def square(k, part):
        if part == 0:
            t_copies[k].wait()
        count = rows // block // parts

        def one(r, _):
            here = pl.ds(pl.multiple_of(r * block, block), block)
            total = None
            for g in range(widths[k] // LANES):
                x = tbufs[k][here, pl.ds(g * LANES, LANES)].astype(jnp.float32)
                total = x * x if total is None else total + x * x
            if k:
                total = total + squares[here, :]
            if k < chunks - 1:
                squares[here, :] = total
            else:
                mean = jnp.sum(total, axis=1, keepdims=True) * jnp.float32(1.0 / width)
                factor = lax.rsqrt(mean + 1e-06) * jnp.float32(width ** -0.5)
                scale[here, :] = jnp.broadcast_to(factor, (block, LANES))

        lax.fori_loop(part * count, (part + 1) * count, one, None)

    def query_block(k, g):
        per = LANES // own
        blocks = [qbufs[k][e % 2, e // 2 % inner, e // 2 // inner] for e in range(g * per, (g + 1) * per)]
        return jnp.concatenate(blocks, axis=0)

    def product(k, here, g):
        return lax.dot_general(
            tbufs[k][here, :], query_block(k, g), (((1,), (1,)), ((), ())),
            preferred_element_type=jnp.float32,
        )

    def multiply(k, part):
        half = rows // 2
        here = pl.ds(part * half, half)

        def one(g):
            new = product(k, here, g)
            acc[g, here, :] = new if k == 0 else acc[g, here, :] + new
        each(groups, one)

    step = 256

    def last(g):
        best = None
        for r in range(rows // step):
            here = pl.ds(r * step, step)
            value = (acc[g, here, :] + product(chunks - 1, here, g)) * scale[here, :]
            for s in range(step // LANES):
                scores_ref[pl.ds(g * LANES, LANES), pl.ds(r * step + s * LANES, LANES)] = (
                    value[s * LANES:(s + 1) * LANES].T
                )
            for s in range(step // 64):
                lists = network([value[s * 64 + i * 8:s * 64 + i * 8 + 8] for i in range(8)], SORT8)
                best = lists if best is None else merge(best, lists)
        tile[g] = over_sublanes(best)

    events = []
    for t in range(chunks + 2):
        events += [(pass_z, t)] * (t < chunks) + [(pass_y, t - 1)] * (0 <= t - 1 < chunks)
        events += [(pass_c, t - 2)] * (0 <= t - 2)
    pending = [(square, k, part) for k in range(chunks) for part in range(parts)]
    for event, k in events:
        event(k)
        if event is pass_c and k < chunks - 1:
            pending += [(multiply, k, 0), (multiply, k, 1)]
        for work, *which in pending[:PER_EVENT]:
            work(*which)
        del pending[:PER_EVENT]
    for work, *which in pending:
        work(*which)
    each(groups, last)

    def tile_copy(i):
        target = lax.rem(me + 1 + i, ex)
        return remote(tile.at[target * own // LANES], tiles.at[me], tile_send.at[i], tile_recv.at[me], target)

    each(ex - 1, lambda i: tile_copy(i).start())
    tiles[me] = tile[me * own // LANES]

    def tile_wait(i):
        source = lax.rem(me + 1 + i, ex)
        arrived(tiles.at[source], tile_recv.at[source])

    each(ex - 1, tile_wait)
    best = None
    for s in range(ex // 8):
        lists = network([tiles[s * 8 + i] for i in range(8)], SORT8)
        best = lists if best is None else merge(best, lists)
    turned[...] = over_sublanes(best).T
    best_ref[...] = turned[pl.ds(pl.multiple_of(lax.rem(me * own, LANES), own), own), :]

    each(ex - 1, lambda i: tile_copy(i).wait_send())
    for k in range(chunks):
        each(outer - 1, lambda i: z_copy(k, i).wait_send())
        each(outer, lambda i: each(inner - 1, lambda j: y_copy(k, i, j).wait_send()))
        each(inner, lambda j: c_copy(k, j).wait_send())


def shards(ex, queries, train_grads):
    own, width = queries.shape
    rows = train_grads.shape[0]
    nq = ex * own
    groups = nq // LANES
    widths = [width * part // sum(SHARES) for part in SHARES]
    chunks = len(widths)
    chips = ex // 2
    inner = 1
    while inner * inner * 4 <= chips:
        inner *= 2
    outer = chips // inner
    any_space = pl.BlockSpec(memory_space=pl.ANY)
    vmem = pl.BlockSpec(memory_space=pltpu.VMEM)
    dma = pltpu.SemaphoreType.DMA
    return pl.pallas_call(
        functools.partial(kernel, outer, inner, widths),
        out_shape=(
            jax.ShapeDtypeStruct((nq, rows), jnp.float32),
            jax.ShapeDtypeStruct((own, TOPV), jnp.float32),
        ),
        in_specs=[any_space, any_space],
        out_specs=(vmem, vmem),
        scratch_shapes=[
            *[pltpu.VMEM((2, inner, outer, own, kc), jnp.bfloat16) for kc in widths],
            *[pltpu.VMEM((rows, kc), jnp.bfloat16) for kc in widths],
            pltpu.VMEM((rows, LANES), jnp.float32),
            pltpu.VMEM((rows, LANES), jnp.float32),
            pltpu.VMEM((groups, rows, LANES), jnp.float32),
            pltpu.VMEM((groups, TOPV, LANES), jnp.float32),
            pltpu.VMEM((ex, TOPV, LANES), jnp.float32),
            pltpu.VMEM((LANES, TOPV), jnp.float32),
            dma((chunks,)),
            dma((chunks,)),
            dma((chunks, max(outer - 1, 1))),
            dma((chunks, outer)),
            dma((chunks, max(inner - 1, 1), outer)),
            dma((chunks, inner, outer)),
            dma((chunks, inner)),
            dma((chunks, inner)),
            dma((ex,)),
            dma((ex,)),
        ],
        compiler_params=pltpu.CompilerParams(
            collective_id=0, has_side_effects=True, vmem_limit_bytes=VMEM_MIB * 1024 * 1024
        ),
    )(queries, train_grads)


def solution(mesh):
    in_specs = (P(("grp", "ex"), None), P(("grp", "ex"), None))
    out_specs = (P(None, ("grp", "ex")), P(("grp", "ex"), None))
    return jax.shard_map(
        functools.partial(shards, mesh.shape["ex"]),
        mesh=mesh, in_specs=in_specs, out_specs=out_specs, check_vma=False,
    )
```

time: 31.1 us -> 27.6 us (0.89)
  Pallas kernels: 28.1 us -> 24.6 us
    pallas_call x1, Pallas kernels: 28.1 us -> 24.6 us  [shards(): pl.pallas_call(functools.partial(kernel, outer, inner, widths), out_shape...]
where the time goes in v2:
time: 27.6 us; the launch traced here: 27.4 us
  Pallas kernels  24.6 us (89%)
  local copies, waits for them, and re-layouts  2.22 us (8%)
  between operations  0.65 us (2%)
    pallas_call x1, Pallas kernels, shards(): pl.pallas_call(functools.partial(kernel, outer, inner, widths), out_shape...  24.6 us
    unnamed x4, local copies, waits for them, and re-layouts  2.22 us

profile of v2, /device:TPU:0, one launch (start us, length us, event | category | flops | bytes accessed | tf_op | source)
XLA Modules:
  0.0 27.4 jit_solution(7044063348864920418)
XLA Ops:
  0.6 0.0 copy-start
  0.6 0.8 %copy-done = bf16[8,4096]{1,0:T(8,128)(2,1)S(1)} copy-done((bf16[8,4096]{1,0:T(8,128)(2,1)S(1)}, bf16[8,4096]{1,0:T(8,128)(2,1)}, u32[]{:S(2)}) %copy-start) | copy-done | bytes 65560
  1.5 24.6 %shard_map.41 = (f32[128,1024]{1,0:T(8,128)S(1)}, f32[8,8]{1,0:T(8,128)S(1)}) custom-call(bf16[8,4096]{1,0:T(8,128)(2,1)S(1)} %copy-done, bf16[1024,4096]{1,0:T(8,128)(2,1)} %t_ref.1), custom_call_target="tpu_custom_call" | custom-call | tf_op jit(solution)/shard_map/pallas_call | solution.py:262
  26.1 0.8 %copy.6 = f32[128,1024]{1,0:T(8,128)} copy(f32[128,1024]{1,0:T(8,128)S(1)} %get-tuple-element.4) | data formatting | bytes 1048576
  26.9 0.6 %copy.7 = f32[8,8]{1,0:T(8,128)} copy(f32[8,8]{1,0:T(8,128)S(1)} %get-tuple-element.5) | data formatting | bytes 512
Async XLA Ops:
  0.6 0.8 %copy-start = (bf16[8,4096]{1,0:T(8,128)(2,1)S(1)}, bf16[8,4096]{1,0:T(8,128)(2,1)}, u32[]{:S(2)}) copy-start(bf16[8,4096]{1,0:T(8,128)(2,1)} %q_ref.1) | copy-start | bytes 196612

commit v3 on v2

--- a/solution.py
+++ b/solution.py
@@ -75,13 +75,14 @@
 
     barrier = pltpu.get_barrier_semaphore()
 
-    def greet(i):
+    def greet(target):
         pl.semaphore_signal(
-            barrier, inc=1, device_id={"ex": lax.rem(me + 1 + i, ex)},
-            device_id_type=pl.DeviceIdType.MESH,
+            barrier, inc=1, device_id={"ex": target}, device_id_type=pl.DeviceIdType.MESH
         )
 
-    each(ex - 1, greet)
+    each(outer - 1, lambda i: greet(at(lax.rem(a + 1 + i, outer), b, core)))
+    each(inner - 1, lambda j: greet(at(a, lax.rem(b + 1 + j, inner), core)))
+    greet(at(a, b, 1 - core))
     t_copies = []
     for k in range(chunks):
         copy = pltpu.make_async_copy(t_ref.at[:, pl.ds(starts[k], widths[k])], tbufs[k], t_sem.at[k])
@@ -92,7 +93,7 @@
         copy = pltpu.make_async_copy(own_block(k), qbufs[k].at[core, b, a], own_sem.at[k])
         copy.start()
         own_copies.append(copy)
-    pl.semaphore_wait(barrier, ex - 1)
+    pl.semaphore_wait(barrier, outer + inner - 1)
 
     def remote(src, dst, send, recv, target):
         return pltpu.make_async_remote_copy(

time: 27.6 us -> 26.1 us (0.946)
  Pallas kernels: 24.6 us -> 23 us
    pallas_call x1, Pallas kernels: 24.6 us -> 23 us  [shards(): pl.pallas_call(functools.partial(kernel, outer, inner, widths), out_shape...]
where the time goes in v3:
time: 26.1 us; the launch traced here: 25.9 us
  Pallas kernels  23 us (88%)
  local copies, waits for them, and re-layouts  2.22 us (9%)
  between operations  0.65 us (2%)
    pallas_call x1, Pallas kernels, shards(): pl.pallas_call(functools.partial(kernel, outer, inner, widths), out_shape...  23 us
    unnamed x4, local copies, waits for them, and re-layouts  2.22 us

profile of v3, /device:TPU:0, one launch (start us, length us, event | category | flops | bytes accessed | tf_op | source)
XLA Modules:
  0.0 25.9 jit_solution(9294749391570648997)
XLA Ops:
  0.6 0.0 copy-start
  0.6 0.8 %copy-done = bf16[8,4096]{1,0:T(8,128)(2,1)S(1)} copy-done((bf16[8,4096]{1,0:T(8,128)(2,1)S(1)}, bf16[8,4096]{1,0:T(8,128)(2,1)}, u32[]{:S(2)}) %copy-start) | copy-done | bytes 65560
  1.5 23.0 %shard_map.41 = (f32[128,1024]{1,0:T(8,128)S(1)}, f32[8,8]{1,0:T(8,128)S(1)}) custom-call(bf16[8,4096]{1,0:T(8,128)(2,1)S(1)} %copy-done, bf16[1024,4096]{1,0:T(8,128)(2,1)} %t_ref.1), custom_call_target="tpu_custom_call" | custom-call | tf_op jit(solution)/shard_map/pallas_call | solution.py:263
  24.5 0.8 %copy.6 = f32[128,1024]{1,0:T(8,128)} copy(f32[128,1024]{1,0:T(8,128)S(1)} %get-tuple-element.4) | data formatting | bytes 1048576
  25.3 0.6 %copy.7 = f32[8,8]{1,0:T(8,128)} copy(f32[8,8]{1,0:T(8,128)S(1)} %get-tuple-element.5) | data formatting | bytes 512
Async XLA Ops:
  0.6 0.8 %copy-start = (bf16[8,4096]{1,0:T(8,128)(2,1)S(1)}, bf16[8,4096]{1,0:T(8,128)(2,1)}, u32[]{:S(2)}) copy-start(bf16[8,4096]{1,0:T(8,128)(2,1)} %q_ref.1) | copy-start | bytes 196612
